TPU v7x, 32 devices: a whole 2x2x4 slice. The times are simulated.
32 devices in a mesh: gx: 4 (over x, core), gy: 8 (over z, y).
Axes of the slice: x: 2, y: 2, z: 4, core: 2. Of those that a mesh axis runs over, the one named last changes fastest.
Arguments:
- start_disp: float32 [3, 128, 256, 128], P(None, 'gx', 'gy'), may hold values from -6 to 6
- start_vel: float32 [3, 128, 256, 128], P(None, 'gx', 'gy'), may hold values from -6 to 6
- stiffness: float32 [128, 256, 128], P('gx', 'gy'), may hold values from 0.5 to 2
- cell_mass: float32 [128, 256, 128], P('gx', 'gy'), may hold values from 0.5 to 2
- contact_cells: int32 [4, 8, 512], P('gx', 'gy'), may hold values from 0 to 1023
- contact_match: int32 [4, 8, 512], P('gx', 'gy'), may hold values from 0 to 511, each once within a row
- eroded_cells: int32 [8, 4, 8, 512], P(None, 'gx', 'gy'), may hold values from 0 to 131071
- owner_ids: int32 [8, 4, 8, 512, 1], P(None, 'gx', 'gy'), may hold values from 0 to 7; in each aligned block of 512 rows (0 to 511, 512 to 1023, ..., all dimensions but the last counted through in order) at most 128 rows name the same one
- bed_position: float32 [4, 8, 3, 1024], P('gx', 'gy'), may hold values from -6 to 6
- bed_velocity: float32 [4, 8, 3, 1024], P('gx', 'gy'), may hold values from -6 to 6
- bed_neighbours: int32 [4, 8, 8, 1024], P('gx', 'gy'), may hold values from 0 to 127
Outputs:
- final_disp: float32 [3, 128, 256, 128], P(None, 'gx', 'gy')
- final_vel: float32 [3, 128, 256, 128], P(None, 'gx', 'gy')
Inputs may be any that keep to these rules, and one draw needn't show every extreme that they name: `owner_ids`: in each step, at most 128 records of one block name one owner, and some block names some owner exactly 128 times.
All inputs are finite; a program needn't handle non-finite values.
Results may differ from a plain program's by a relative error of at most 0.0001.
Values sent between devices are 32-bit elements; how exact they have to be, the bound alone decides.
A program may use at most 128 MiB of HBM per device.

v0:
```python
import functools

import jax
import jax.numpy as jnp
from jax import lax
from jax.experimental import pallas as pl
from jax.experimental.pallas import tpu as pltpu
from jax.sharding import PartitionSpec as P

TIME_STEP = 0.2
CONTACT_K = 0.5
PARTICLE_K = 1.0
DRAG_COEF = 0.5
LANES = 128
F32 = jnp.float32
BF16 = jnp.bfloat16
MESH = pl.DeviceIdType.MESH


def take_lanes(x, idx):
    return jnp.take_along_axis(x, idx, axis=1, mode="promise_in_bounds")


def dot_nt(a, b):
    return lax.dot_general(a, b, (((1,), (1,)), ((), ())), preferred_element_type=F32)


def two_parts(x):
    hi = x.astype(BF16).astype(F32)
    return hi, x - hi


def rows8(row):
    return jnp.broadcast_to(row, (8, row.shape[1]))


def kernel(
    dims,
    cells_s, contact_s, disp_in, vel_in, stiff_in, mass_in, contact_v, match_v, cells_v, owner_v, bpos, bvel, bnbr,
    disp_out, vel_out,
    D, V, A, G, top_add, ye, yh, xh, msg, rx, ans, ax, seg, ps, inv, rank, part, nbr, nbr_hot, seg_hot, b_hi, b_lo,
    out_sem, ye_send, yh_recv, xe_send, xh_recv, m_send, m_recv, a_send, a_recv, p_send, p_recv,
):
    n_gx, n_gy, cx, cy, steps, n_rec, n_seg, n_blocks, n_nbr = dims
    n_cols = cx * cy
    group = LANES // n_gy
    rec_tiles = n_rec // LANES
    seg_tiles = n_seg // LANES
    chunk_x = 8
    chunk = chunk_x * cy
    a = lax.axis_index("gx")
    b = lax.axis_index("gy")
    mate = a + 1 - 2 * lax.rem(a, 2)
    lane = lax.broadcasted_iota(jnp.int32, (8, LANES), 1)
    sub = lax.broadcasted_iota(jnp.int32, (8, LANES), 0)

    flat = G.reshape(n_cols * 8, LANES)

    yh[...] = jnp.zeros_like(yh)
    xh[...] = jnp.zeros_like(xh)

    def init_chunk(i, _):
        x0 = i * chunk_x
        xs = pl.ds(x0, chunk_x)
        m = mass_in[xs].reshape(chunk, LANES)
        A[xs] = TIME_STEP * stiff_in[xs] / mass_in[xs]
        base = pl.multiple_of(i * (chunk * 8), chunk * 8)
        for f in range(3):
            d = disp_in[f, xs]
            v = vel_in[f, xs]
            D[f, pl.ds(x0 + 1, chunk_x)] = d
            V[f, xs] = v
            flat[pl.ds(base + f, chunk, stride=8), :] = d.reshape(chunk, LANES)
            flat[pl.ds(base + 3 + f, chunk, stride=8), :] = v.reshape(chunk, LANES)
            for xx in range(chunk_x):
                ye[0, f, pl.ds(x0 + xx, 1), :] = d[xx, 0:1]
                ye[1, f, pl.ds(x0 + xx, 1), :] = d[xx, cy - 1:cy]
        flat[pl.ds(base + 6, chunk, stride=8), :] = m
        flat[pl.ds(base + 7, chunk, stride=8), :] = jnp.zeros_like(m)
        cols = lax.broadcasted_iota(jnp.int32, (chunk, n_seg), 0) + i * chunk
        seg_hot[pl.ds(pl.multiple_of(i * chunk, chunk), chunk), :] = jnp.where(cols == contact_v[...], 1.0, 0.0).astype(BF16)
        return 0

    lax.fori_loop(0, cx // chunk_x, init_chunk, 0)

    tri = jnp.where(
        lax.broadcasted_iota(jnp.int32, (n_rec, n_rec), 1) <= lax.broadcasted_iota(jnp.int32, (n_rec, n_rec), 0), 1.0, 0.0
    ).astype(BF16)

    def init_step(s, _):
        own = owner_v[pl.ds(s, 1), :]
        mine = lax.broadcasted_iota(jnp.int32, (n_gy, n_rec), 0) == own
        hot = jnp.where(mine, 1.0, 0.0)
        counted = dot_nt(jnp.concatenate([hot] * 2, axis=0).astype(BF16), tri)[:n_gy]
        rk = (jnp.sum(hot * counted, axis=0, keepdims=True) - 1.0).astype(jnp.int32)
        rank[pl.ds(s, 1), :] = rk
        rec = lax.broadcasted_iota(jnp.int32, (n_gy, n_rec), 1) + 1
        lo = jnp.where(mine, (rec & 127).astype(F32), 0.0)
        hi = jnp.where(mine, (rec >> 7).astype(F32), 0.0)
        q_hot = jnp.where(lax.broadcasted_iota(jnp.int32, (LANES, n_rec), 0) == rk, 1.0, 0.0).astype(BF16)
        both = dot_nt(jnp.concatenate([lo, hi], axis=0).astype(BF16), q_hot)
        inv[s] = (both[:n_gy] + 128.0 * both[n_gy:]).astype(jnp.int32) - 1
        return 0

    lax.fori_loop(0, steps, init_step, 0)

    perm = lax.rem(lane, group) * n_gy + lane // group
    nrow = lax.broadcasted_iota(jnp.int32, (LANES, LANES), 0)

    def init_block(j, _):
        at = pl.ds(pl.multiple_of(j * LANES, LANES), LANES)
        rows = jnp.concatenate([bpos[:, at], bvel[:, at], jnp.zeros((2, LANES), F32)], axis=0)
        part[j] = take_lanes(rows, perm)
        old = take_lanes(bnbr[:, at], perm)
        new = lax.rem(old, n_gy) * group + old // n_gy
        nbr[j] = new
        for k in range(n_nbr):
            nbr_hot[j, pl.ds(k * LANES, LANES), :] = jnp.where(nrow == new[k:k + 1], 1.0, 0.0).astype(BF16)
        return 0

    lax.fori_loop(0, n_blocks, init_block, 0)

    barrier = pltpu.get_barrier_semaphore()
    for k in range(1, n_gy):
        pl.semaphore_signal(barrier, inc=1, device_id=(a, lax.rem(b + k, n_gy)), device_id_type=MESH)

    @pl.when(a > 0)
    def _():
        pl.semaphore_signal(barrier, inc=1, device_id=(a - 1, b), device_id_type=MESH)

    @pl.when(a < n_gx - 1)
    def _():
        pl.semaphore_signal(barrier, inc=1, device_id=(a + 1, b), device_id_type=MESH)

    near = jnp.where(a > 0, 1, 0) + jnp.where(a < n_gx - 1, 1, 0)
    pl.semaphore_wait(barrier, n_gy - 1 + near)

    def remote(src, dst, send, recv, to):
        return pltpu.make_async_remote_copy(src_ref=src, dst_ref=dst, send_sem=send, recv_sem=recv, device_id=to, device_id_type=MESH)

    def step(s, _):
        p = lax.rem(s, 2)
        halos = (
            (a > 0, remote(D.at[:, 1], xh.at[p, 1], xe_send.at[0], xh_recv.at[p, 1], (a - 1, b)), 0),
            (a < n_gx - 1, remote(D.at[:, cx], xh.at[p, 0], xe_send.at[1], xh_recv.at[p, 0], (a + 1, b)), 1),
        )
        y_halos = (
            (b > 0, remote(ye.at[0], yh.at[p, 1], ye_send.at[0], yh_recv.at[p, 1], (a, b - 1)), 0),
            (b < n_gy - 1, remote(ye.at[1], yh.at[p, 0], ye_send.at[1], yh_recv.at[p, 0], (a, b + 1)), 1),
        )

        def read_tile(scalar, lane_of):
            def body(i, acc):
                for u in range(8):
                    t = i * 8 + u
                    col, z = lane_of(scalar(t))
                    acc = jnp.where(lane == t, take_lanes(G[col], jnp.full((8, LANES), z, jnp.int32)), acc)
                return acc

            return lax.fori_loop(0, LANES // 8, body, jnp.zeros((8, LANES), F32))

        recs = [
            read_tile(lambda t, w=w: cells_s[s, w * LANES + t], lambda c: (c >> 7, c & 127))
            for w in range(rec_tiles)
        ]
        for o in range(n_gy):
            idx = rows8(inv[s, o:o + 1, :])
            out = jnp.zeros((8, LANES), F32)
            for w in range(rec_tiles):
                out = jnp.where((idx >> 7) == w, take_lanes(recs[w], idx & 127), out)
            msg[o] = out
        rx[p, b] = msg[b]
        m_copies = []
        for k in range(1, n_gy):
            o = lax.rem(b + k, n_gy)
            m_copies.append(remote(msg.at[o], rx.at[p, b], m_send.at[k], m_recv.at[p, b], (a, o)))
            m_copies[-1].start()
        for there, copy, _k in halos + y_halos:
            @pl.when(there)
            def _(copy=copy):
                copy.start()

        segs = [
            read_tile(lambda t, w=w: contact_s[0, w * LANES + t], lambda c: (c, LANES - 1)) for w in range(seg_tiles)
        ]
        for w in range(seg_tiles):
            seg[w] = segs[w]
        p_copy = remote(seg, ps.at[p], p_send, p_recv.at[p], (mate, b))
        p_copy.start()

        def wait_from(dst, recv):
            pltpu.make_async_copy(dst, dst, recv).wait()

        @pl.when(a > 0)
        def _():
            wait_from(xh.at[p, 0], xh_recv.at[p, 0])

        @pl.when(a < n_gx - 1)
        def _():
            wait_from(xh.at[p, 1], xh_recv.at[p, 1])

        @pl.when(b > 0)
        def _():
            wait_from(yh.at[p, 0], yh_recv.at[p, 0])

        @pl.when(b < n_gy - 1)
        def _():
            wait_from(yh.at[p, 1], yh_recv.at[p, 1])

        D[:, 0] = xh[p, 0]
        D[:, cx + 1] = xh[p, 1]
        wait_from(ps.at[p], p_recv.at[p])
        c_parts = [[], []]
        for w in range(seg_tiles):
            idx = rows8(match_v[:, w * LANES:(w + 1) * LANES])
            facing = jnp.zeros((8, LANES), F32)
            for u in range(seg_tiles):
                facing = jnp.where((idx >> 7) == u, take_lanes(ps[p, u], idx & 127), facing)
            pull = (TIME_STEP * CONTACT_K) * (facing - segs[w]) / segs[w][6:7]
            hi, lo = two_parts(pull)
            c_parts[0].append(hi)
            c_parts[1].append(lo)
        zero_rows = jnp.zeros((LANES - 8, n_seg), F32)
        c_mats = [jnp.concatenate([jnp.concatenate(part_, axis=1), zero_rows], axis=0).astype(BF16) for part_ in c_parts]

        def top_chunk(i, _):
            at = pl.ds(pl.multiple_of(i * chunk, chunk), chunk)
            hot = seg_hot[at, :]
            top_add[at, :] = dot_nt(hot, c_mats[0]) + dot_nt(hot, c_mats[1])
            return 0

        lax.fori_loop(0, cx // chunk_x, top_chunk, 0)

        row_i = lax.broadcasted_iota(jnp.int32, (cy, LANES), 0)
        lane_i = lax.broadcasted_iota(jnp.int32, (cy, LANES), 1)

        def lap_row(x, _):
            top = top_add[pl.ds(pl.multiple_of(x * cy, cy), cy), :]
            scale = A[x]
            for f in range(3):
                c = D[f, x + 1]
                lap = D[f, x] + D[f, x + 2] - 6.0 * c
                lap += jnp.where(row_i == 0, yh[p, 0, f, pl.ds(x, 1), :], pltpu.roll(c, 1, 0))
                lap += jnp.where(row_i == cy - 1, yh[p, 1, f, pl.ds(x, 1), :], pltpu.roll(c, cy - 1, 0))
                lap += jnp.where(lane_i == 0, 0.0, pltpu.roll(c, 1, 1))
                lap += jnp.where(lane_i == LANES - 1, 0.0, pltpu.roll(c, LANES - 1, 1))
                push = jnp.where(lane_i == LANES - 1, pltpu.roll(top, LANES - 1 - f, 1), 0.0)
                V[f, x] = V[f, x] + scale * lap + push
            return 0

        lax.fori_loop(0, cx, lap_row, 0)

        for k in range(1, n_gy):
            src = lax.rem(b + k, n_gy)
            wait_from(rx.at[p, src], m_recv.at[p, src])
        got = [rx[p, src] for src in range(n_gy)]
        replies = [jnp.zeros((8, LANES), F32) for _ in range(n_gy)]
        springs = []
        for j in range(n_blocks):
            rec = jnp.zeros((8, LANES), F32)
            for src in range(n_gy):
                moved = pltpu.roll(got[src], ((src - j) * group) % LANES, 1) if src != j else got[src]
                rec = jnp.where(lane // group == src, moved, rec)
            idx = nbr[j]
            state = part[j]
            diff = [take_lanes(rows8(state[f:f + 1]), idx) - rec[f:f + 1] for f in range(6)]
            gain = rec[6:7] / (1.0 + diff[0] * diff[0] + diff[1] * diff[1] + diff[2] * diff[2])
            force = jnp.zeros((8, LANES), F32)
            for f in range(3):
                spring = gain * (PARTICLE_K * diff[f])
                springs.append(spring)
                total = jnp.sum(spring + gain * (DRAG_COEF * diff[3 + f]), axis=0, keepdims=True)
                force = jnp.where(sub == f, total, force)
            force = force * (1.0 / n_nbr)
            for src in range(n_gy):
                moved = pltpu.roll(force, ((j - src) * group) % LANES, 1) if src != j else force
                replies[src] = jnp.where(lane // group == j, moved, replies[src])
        for src in range(n_gy):
            ans[src] = replies[src]
        ax[p, b] = ans[b]
        a_copies = []
        for k in range(1, n_gy):
            o = lax.rem(b + k, n_gy)
            a_copies.append(remote(ans.at[o], ax.at[p, b], a_send.at[k], a_recv.at[p, b], (a, o)))
            a_copies[-1].start()

        for j in range(n_blocks):
            parts = [two_parts(springs[3 * j + f]) for f in range(3)]
            lhs = jnp.concatenate([q[0] for q in parts] + [q[1] for q in parts], axis=0).astype(BF16)
            wide = dot_nt(lhs, nbr_hot[j])
            change = jnp.zeros((8, LANES), F32)
            for f in range(3):
                acc = jnp.zeros((8, LANES), F32)
                for k in range(n_nbr):
                    ks = slice(k * LANES, (k + 1) * LANES)
                    acc = jnp.where(sub == k, wide[8 * f:8 * f + 8, ks] + wide[24 + 8 * f:32 + 8 * f, ks], acc)
                total = jnp.sum(acc, axis=0, keepdims=True) * (-TIME_STEP / n_nbr)
                change = change + jnp.where(sub == 3 + f, total, 0.0)
            state = part[j] + change
            part[j] = state + jnp.where(sub < 3, TIME_STEP * pltpu.roll(state, 5, 0), 0.0)

        for k in range(1, n_gy):
            src = lax.rem(b + k, n_gy)
            wait_from(ax.at[p, src], a_recv.at[p, src])
        cell_row = cells_v[pl.ds(s, 1), :]
        own_row = owner_v[pl.ds(s, 1), :]
        rank_row = rank[pl.ds(s, 1), :]
        zrow = lax.broadcasted_iota(jnp.int32, (LANES, LANES), 0)
        for w in range(rec_tiles):
            ws = slice(w * LANES, (w + 1) * LANES)
            own8, rank8 = rows8(own_row[:, ws]), rows8(rank_row[:, ws])
            force = jnp.zeros((8, LANES), F32)
            for o in range(n_gy):
                force = jnp.where(own8 == o, take_lanes(ax[p, o], rank8), force)
            push = TIME_STEP * force / recs[w][6:7]
            hi, lo = two_parts(push)
            here = zrow == (cell_row[:, ws] & 127)
            for f in range(3):
                b_hi[f * LANES:(f + 1) * LANES, ws] = jnp.where(here, hi[f:f + 1], 0.0).astype(BF16)
                b_lo[f * LANES:(f + 1) * LANES, ws] = jnp.where(here, lo[f:f + 1], 0.0).astype(BF16)
        for copy in m_copies + a_copies + [p_copy]:
            copy.wait_send()
        for there, copy, _k in halos + y_halos:
            @pl.when(there)
            def _(copy=copy):
                copy.wait_send()

        col_row = cell_row >> 7

        def add_chunk(i, _):
            x0 = i * chunk_x
            cols = lax.broadcasted_iota(jnp.int32, (chunk, n_rec), 0) + i * chunk
            hot = jnp.where(cols == col_row, 1.0, 0.0).astype(BF16)
            base = pl.multiple_of(i * (chunk * 8), chunk * 8)
            for f in range(3):
                fs = pl.ds(f * LANES, LANES)
                add = dot_nt(hot, b_hi[fs, :]) + dot_nt(hot, b_lo[fs, :])
                v = V[f, pl.ds(x0, chunk_x)].reshape(chunk, LANES) + add
                d = D[f, pl.ds(x0 + 1, chunk_x)].reshape(chunk, LANES) + TIME_STEP * v
                V[f, pl.ds(x0, chunk_x)] = v.reshape(chunk_x, cy, LANES)
                D[f, pl.ds(x0 + 1, chunk_x)] = d.reshape(chunk_x, cy, LANES)
                flat[pl.ds(base + f, chunk, stride=8), :] = d
                flat[pl.ds(base + 3 + f, chunk, stride=8), :] = v
                for xx in range(chunk_x):
                    ye[0, f, pl.ds(x0 + xx, 1), :] = d[xx * cy:xx * cy + 1]
                    ye[1, f, pl.ds(x0 + xx, 1), :] = d[xx * cy + cy - 1:xx * cy + cy]
            return 0

        lax.fori_loop(0, cx // chunk_x, add_chunk, 0)
        return 0

    lax.fori_loop(0, steps, step, 0)
    out_d = pltpu.make_async_copy(D.at[:, pl.ds(1, cx)], disp_out, out_sem.at[0])
    out_v = pltpu.make_async_copy(V, vel_out, out_sem.at[1])
    out_d.start()
    out_v.start()
    out_d.wait()
    out_v.wait()


def local(n_gx, n_gy, disp, vel, stiff, mass, contact_cells, contact_match, eroded, owners, bpos, bvel, bnbr):
    cx, cy, nz = disp.shape[1:]
    steps, n_rec = eroded.shape[0], eroded.shape[3]
    n_seg = contact_cells.shape[2]
    n_slots = bpos.shape[3]
    n_blocks = n_slots // LANES
    n_nbr = bnbr.shape[2]
    dims = (n_gx, n_gy, cx, cy, steps, n_rec, n_seg, n_blocks, n_nbr)
    contact = contact_cells.reshape(1, n_seg)
    cells = eroded.reshape(steps, n_rec)
    vm = pl.BlockSpec(memory_space=pltpu.VMEM)
    sm = pl.BlockSpec(memory_space=pltpu.SMEM)
    dma = pltpu.SemaphoreType.DMA
    tile = (8, LANES)
    return pl.pallas_call(
        functools.partial(kernel, dims),
        out_shape=(jax.ShapeDtypeStruct(disp.shape, F32), jax.ShapeDtypeStruct(vel.shape, F32)),
        in_specs=[sm, sm] + [vm] * 11,
        out_specs=(pl.BlockSpec(memory_space=pl.ANY), pl.BlockSpec(memory_space=pl.ANY)),
        scratch_shapes=[
            pltpu.VMEM((3, cx + 2, cy, nz), F32),
            pltpu.VMEM((3, cx, cy, nz), F32),
            pltpu.VMEM((cx, cy, nz), F32),
            pltpu.VMEM((cx * cy, 8, nz), F32),
            pltpu.VMEM((cx * cy, nz), F32),
            pltpu.VMEM((2, 3, cx, nz), F32),
            pltpu.VMEM((2, 2, 3, cx, nz), F32),
            pltpu.VMEM((2, 2, 3, cy, nz), F32),
            pltpu.VMEM((n_gy,) + tile, F32),
            pltpu.VMEM((2, n_gy) + tile, F32),
            pltpu.VMEM((n_gy,) + tile, F32),
            pltpu.VMEM((2, n_gy) + tile, F32),
            pltpu.VMEM((n_seg // LANES,) + tile, F32),
            pltpu.VMEM((2, n_seg // LANES) + tile, F32),
            pltpu.VMEM((steps, n_gy, LANES), jnp.int32),
            pltpu.VMEM((steps, n_rec), jnp.int32),
            pltpu.VMEM((n_blocks,) + tile, F32),
            pltpu.VMEM((n_blocks,) + tile, jnp.int32),
            pltpu.VMEM((n_blocks, n_nbr * LANES, LANES), BF16),
            pltpu.VMEM((cx * cy, n_seg), BF16),
            pltpu.VMEM((3 * LANES, n_rec), BF16),
            pltpu.VMEM((3 * LANES, n_rec), BF16),
            dma((2,)),
            dma((2,)), dma((2, 2)),
            dma((2,)), dma((2, 2)),
            dma((n_gy,)), dma((2, n_gy)),
            dma((n_gy,)), dma((2, n_gy)),
            dma, dma((2,)),
        ],
        compiler_params=pltpu.CompilerParams(collective_id=0, has_side_effects=True, vmem_limit_bytes=48 * 2**20),
        name="dynamics",
    )(
        cells, contact, disp, vel, stiff, mass, contact, contact_match.reshape(1, n_seg), cells,
        owners.reshape(steps, n_rec), bpos[0, 0], bvel[0, 0], bnbr[0, 0],
    )


def solution(mesh):
    return jax.shard_map(
        functools.partial(local, mesh.shape["gx"], mesh.shape["gy"]),
        mesh=mesh,
        in_specs=(
            P(None, "gx", "gy", None),
            P(None, "gx", "gy", None),
            P("gx", "gy", None),
            P("gx", "gy", None),
            P("gx", "gy", None),
            P("gx", "gy", None),
            P(None, "gx", "gy", None),
            P(None, "gx", "gy", None, None),
            P("gx", "gy", None, None),
            P("gx", "gy", None, None),
            P("gx", "gy", None, None),
        ),
        out_specs=(P(None, "gx", "gy", None), P(None, "gx", "gy", None)),
        check_vma=False,
    )
```

profile of v0, /device:TPU:0, one launch (start us, length us, event | category | flops | bytes accessed | tf_op | source)
XLA Modules:
  0.0 213.7 jit_solution(2686567316363566423)
XLA Ops:
  0.6 0.7 copy.22
  1.3 0.7 copy.21
  2.1 0.7 copy_bitcast_fusion
  2.8 0.0 copy-start
  2.8 1.4 copy-done
  4.2 0.0 copy-start.1
  4.2 1.0 copy-done.1
  5.3 0.0 copy-start.2
  5.3 1.0 copy-done.2
  6.3 0.0 copy-start.3
  6.3 0.8 copy-done.3
  7.1 0.0 copy-start.4
  7.1 0.7 copy-done.4
  7.7 0.0 copy-start.5
  7.7 0.7 copy-done.5
  8.4 203.0 %dynamics.1 = (f32[3,32,32,128]{3,2,1,0:T(8,128)S(1)}, f32[3,32,32,128]{3,2,1,0:T(8,128)S(1)}) custom-call(s32[8,512]{1,0:T(8,128)S(1)} %bitcast.13, s32[1,512]{1,0:T(1,128)S(1)} %bitcast.17, f32[3,32,32,128]{3,2,1,0:T(8,128)S(1)} %copy-done, f32[3,32,32,128]{3,2,1,0:T(8,128)} %vel_in.1, f32[32,32,128]{2,1,0:T(8,128)S(1)} %copy-done.1, ...), custom_call_target="tpu_custom_call" | custom-call | tf_op jit(solution)/shard_map/dynamics/pallas_call | solution.py:375
  211.4 1.1 copy.25
  212.6 1.1 copy.26
Async XLA Ops:
  2.8 1.4 copy-start
  4.2 1.0 copy-start.1
  5.3 1.0 copy-start.2
  6.3 0.8 copy-start.3
  7.1 0.7 copy-start.4
  7.7 0.7 copy-start.5
where the time goes:
time: 214 us
  Pallas kernels  203 us (95%)
  local copies, waits for them, and re-layouts  10.1 us (5%)
    pallas_call x1, Pallas kernels, local(): pl.pallas_call(functools.partial(kernel, dims), out_shape=(jax.ShapeDtype...  203 us
    unnamed x17, local copies, waits for them, and re-layouts  10.1 us

commit v1 on v0

--- a/solution.py
+++ b/solution.py
@@ -38,8 +38,8 @@
     dims,
     cells_s, contact_s, disp_in, vel_in, stiff_in, mass_in, contact_v, match_v, cells_v, owner_v, bpos, bvel, bnbr,
     disp_out, vel_out,
-    D, V, A, G, top_add, ye, yh, xh, msg, rx, ans, ax, seg, ps, inv, rank, part, nbr, nbr_hot, seg_hot, b_hi, b_lo,
-    out_sem, ye_send, yh_recv, xe_send, xh_recv, m_send, m_recv, a_send, a_recv, p_send, p_recv,
+    D, V, A, M, G, recs_buf, near, rec_hot, top_add, ye, yh, xh, msg, rx, ans, ax, seg, ps, inv, rank, part, nbr, nbr_hot, seg_hot, b_both,
+    out_sem, in_sem, ye_send, yh_recv, xe_send, xh_recv, m_send, m_recv, a_send, a_recv, p_send, p_recv,
 ):
     n_gx, n_gy, cx, cy, steps, n_rec, n_seg, n_blocks, n_nbr = dims
     n_cols = cx * cy
@@ -56,39 +56,24 @@
 
     flat = G.reshape(n_cols * 8, LANES)
 
+    loads = [
+        pltpu.make_async_copy(disp_in, D.at[:, pl.ds(1, cx)], in_sem.at[0]),
+        pltpu.make_async_copy(vel_in, V, in_sem.at[1]),
+        pltpu.make_async_copy(stiff_in, A, in_sem.at[2]),
+        pltpu.make_async_copy(mass_in, M, in_sem.at[3]),
+    ]
+    for load in loads:
+        load.start()
     yh[...] = jnp.zeros_like(yh)
     xh[...] = jnp.zeros_like(xh)
 
-    def init_chunk(i, _):
-        x0 = i * chunk_x
-        xs = pl.ds(x0, chunk_x)
-        m = mass_in[xs].reshape(chunk, LANES)
-        A[xs] = TIME_STEP * stiff_in[xs] / mass_in[xs]
-        base = pl.multiple_of(i * (chunk * 8), chunk * 8)
-        for f in range(3):
-            d = disp_in[f, xs]
-            v = vel_in[f, xs]
-            D[f, pl.ds(x0 + 1, chunk_x)] = d
-            V[f, xs] = v
-            flat[pl.ds(base + f, chunk, stride=8), :] = d.reshape(chunk, LANES)
-            flat[pl.ds(base + 3 + f, chunk, stride=8), :] = v.reshape(chunk, LANES)
-            for xx in range(chunk_x):
-                ye[0, f, pl.ds(x0 + xx, 1), :] = d[xx, 0:1]
-                ye[1, f, pl.ds(x0 + xx, 1), :] = d[xx, cy - 1:cy]
-        flat[pl.ds(base + 6, chunk, stride=8), :] = m
-        flat[pl.ds(base + 7, chunk, stride=8), :] = jnp.zeros_like(m)
-        cols = lax.broadcasted_iota(jnp.int32, (chunk, n_seg), 0) + i * chunk
-        seg_hot[pl.ds(pl.multiple_of(i * chunk, chunk), chunk), :] = jnp.where(cols == contact_v[...], 1.0, 0.0).astype(BF16)
-        return 0
-
-    lax.fori_loop(0, cx // chunk_x, init_chunk, 0)
 
     tri = jnp.where(
         lax.broadcasted_iota(jnp.int32, (n_rec, n_rec), 1) <= lax.broadcasted_iota(jnp.int32, (n_rec, n_rec), 0), 1.0, 0.0
     ).astype(BF16)
 
     def init_step(s, _):
-        own = owner_v[pl.ds(s, 1), :]
+        own = owner_v[s, 0]
         mine = lax.broadcasted_iota(jnp.int32, (n_gy, n_rec), 0) == own
         hot = jnp.where(mine, 1.0, 0.0)
         counted = dot_nt(jnp.concatenate([hot] * 2, axis=0).astype(BF16), tri)[:n_gy]
@@ -120,6 +105,31 @@
 
     lax.fori_loop(0, n_blocks, init_block, 0)
 
+    for load in loads:
+        load.wait()
+
+    def init_chunk(i, _):
+        x0 = i * chunk_x
+        xs = pl.ds(x0, chunk_x)
+        m = M[xs].reshape(chunk, LANES)
+        A[xs] = TIME_STEP * A[xs] / M[xs]
+        base = pl.multiple_of(i * (chunk * 8), chunk * 8)
+        for f in range(3):
+            d = D[f, pl.ds(x0 + 1, chunk_x)]
+            v = V[f, xs]
+            flat[pl.ds(base + f, chunk, stride=8), :] = d.reshape(chunk, LANES)
+            flat[pl.ds(base + 3 + f, chunk, stride=8), :] = v.reshape(chunk, LANES)
+            for xx in range(chunk_x):
+                ye[0, f, pl.ds(x0 + xx, 1), :] = d[xx, 0:1]
+                ye[1, f, pl.ds(x0 + xx, 1), :] = d[xx, cy - 1:cy]
+        flat[pl.ds(base + 6, chunk, stride=8), :] = m
+        flat[pl.ds(base + 7, chunk, stride=8), :] = jnp.zeros_like(m)
+        cols = lax.broadcasted_iota(jnp.int32, (chunk, n_seg), 0) + i * chunk
+        seg_hot[pl.ds(pl.multiple_of(i * chunk, chunk), chunk), :] = jnp.where(cols == contact_v[...], 1.0, 0.0).astype(BF16)
+        return 0
+
+    lax.fori_loop(0, cx // chunk_x, init_chunk, 0)
+
     barrier = pltpu.get_barrier_semaphore()
     for k in range(1, n_gy):
         pl.semaphore_signal(barrier, inc=1, device_id=(a, lax.rem(b + k, n_gy)), device_id_type=MESH)
@@ -132,8 +142,8 @@
     def _():
         pl.semaphore_signal(barrier, inc=1, device_id=(a + 1, b), device_id_type=MESH)
 
-    near = jnp.where(a > 0, 1, 0) + jnp.where(a < n_gx - 1, 1, 0)
-    pl.semaphore_wait(barrier, n_gy - 1 + near)
+    n_near = jnp.where(a > 0, 1, 0) + jnp.where(a < n_gx - 1, 1, 0)
+    pl.semaphore_wait(barrier, n_gy - 1 + n_near)
 
     def remote(src, dst, send, recv, to):
         return pltpu.make_async_remote_copy(src_ref=src, dst_ref=dst, send_sem=send, recv_sem=recv, device_id=to, device_id_type=MESH)
@@ -149,20 +159,21 @@
             (b < n_gy - 1, remote(ye.at[1], yh.at[p, 0], ye_send.at[1], yh_recv.at[p, 0], (a, b + 1)), 1),
         )
 
-        def read_tile(scalar, lane_of):
-            def body(i, acc):
-                for u in range(8):
-                    t = i * 8 + u
-                    col, z = lane_of(scalar(t))
-                    acc = jnp.where(lane == t, take_lanes(G[col], jnp.full((8, LANES), z, jnp.int32)), acc)
-                return acc
-
-            return lax.fori_loop(0, LANES // 8, body, jnp.zeros((8, LANES), F32))
-
-        recs = [
-            read_tile(lambda t, w=w: cells_s[s, w * LANES + t], lambda c: (c >> 7, c & 127))
-            for w in range(rec_tiles)
-        ]
+        for there, copy, _k in halos + y_halos:
+            @pl.when(there)
+            def _(copy=copy):
+                copy.start()
+
+        def read_rec(w, _):
+            acc = jnp.zeros((8, LANES), F32)
+            for t in range(LANES):
+                cell = cells_s[s, 0, 0, w * LANES + t]
+                acc = jnp.where(lane == t, take_lanes(G[cell >> 7], jnp.full((8, LANES), cell & 127, jnp.int32)), acc)
+            recs_buf[w] = acc
+            return 0
+
+        lax.fori_loop(0, rec_tiles, read_rec, 0)
+        recs = [recs_buf[w] for w in range(rec_tiles)]
         for o in range(n_gy):
             idx = rows8(inv[s, o:o + 1, :])
             out = jnp.zeros((8, LANES), F32)
@@ -175,16 +186,14 @@
             o = lax.rem(b + k, n_gy)
             m_copies.append(remote(msg.at[o], rx.at[p, b], m_send.at[k], m_recv.at[p, b], (a, o)))
             m_copies[-1].start()
-        for there, copy, _k in halos + y_halos:
-            @pl.when(there)
-            def _(copy=copy):
-                copy.start()
-
-        segs = [
-            read_tile(lambda t, w=w: contact_s[0, w * LANES + t], lambda c: (c, LANES - 1)) for w in range(seg_tiles)
-        ]
-        for w in range(seg_tiles):
-            seg[w] = segs[w]
+        def read_seg(w, _):
+            acc = jnp.zeros((8, LANES), F32)
+            for t in range(LANES):
+                acc = jnp.where(lane == t, pltpu.roll(G[contact_s[0, w * LANES + t]], (t + 1) % LANES, 1), acc)
+            seg[w] = acc
+            return 0
+
+        lax.fori_loop(0, seg_tiles, read_seg, 0)
         p_copy = remote(seg, ps.at[p], p_send, p_recv.at[p], (mate, b))
         p_copy.start()
 
@@ -216,12 +225,13 @@
             facing = jnp.zeros((8, LANES), F32)
             for u in range(seg_tiles):
                 facing = jnp.where((idx >> 7) == u, take_lanes(ps[p, u], idx & 127), facing)
-            pull = (TIME_STEP * CONTACT_K) * (facing - segs[w]) / segs[w][6:7]
-            hi, lo = two_parts(pull)
+            own = seg[w]
+            pull = (TIME_STEP * CONTACT_K) * (facing - own) / own[6:7]
+            hi, lo = two_parts(pltpu.roll(jnp.where(sub < 3, pull, 0.0), 5, 0))
             c_parts[0].append(hi)
             c_parts[1].append(lo)
         zero_rows = jnp.zeros((LANES - 8, n_seg), F32)
-        c_mats = [jnp.concatenate([jnp.concatenate(part_, axis=1), zero_rows], axis=0).astype(BF16) for part_ in c_parts]
+        c_mats = [jnp.concatenate([zero_rows, jnp.concatenate(part_, axis=1)], axis=0).astype(BF16) for part_ in c_parts]
 
         def top_chunk(i, _):
             at = pl.ds(pl.multiple_of(i * chunk, chunk), chunk)
@@ -234,7 +244,7 @@
         row_i = lax.broadcasted_iota(jnp.int32, (cy, LANES), 0)
         lane_i = lax.broadcasted_iota(jnp.int32, (cy, LANES), 1)
 
-        def lap_row(x, _):
+        def lap_row(x):
             top = top_add[pl.ds(pl.multiple_of(x * cy, cy), cy), :]
             scale = A[x]
             for f in range(3):
@@ -244,11 +254,20 @@
                 lap += jnp.where(row_i == cy - 1, yh[p, 1, f, pl.ds(x, 1), :], pltpu.roll(c, cy - 1, 0))
                 lap += jnp.where(lane_i == 0, 0.0, pltpu.roll(c, 1, 1))
                 lap += jnp.where(lane_i == LANES - 1, 0.0, pltpu.roll(c, LANES - 1, 1))
-                push = jnp.where(lane_i == LANES - 1, pltpu.roll(top, LANES - 1 - f, 1), 0.0)
+                push = jnp.where(lane_i == LANES - 1, pltpu.roll(top, 2 - f, 1) if f < 2 else top, 0.0)
                 V[f, x] = V[f, x] + scale * lap + push
-            return 0
-
-        lax.fori_loop(0, cx, lap_row, 0)
+
+        def lap_rows(i, _):
+            lap_row(2 * i)
+            lap_row(2 * i + 1)
+            return 0
+
+        lax.fori_loop(0, cx // 4, lap_rows, 0)
+        for j in range(n_blocks):
+            state = part[j]
+            idx = nbr[j]
+            for f in range(6):
+                near[j, f] = take_lanes(rows8(state[f:f + 1]), idx)
 
         for k in range(1, n_gy):
             src = lax.rem(b + k, n_gy)
@@ -261,9 +280,7 @@
             for src in range(n_gy):
                 moved = pltpu.roll(got[src], ((src - j) * group) % LANES, 1) if src != j else got[src]
                 rec = jnp.where(lane // group == src, moved, rec)
-            idx = nbr[j]
-            state = part[j]
-            diff = [take_lanes(rows8(state[f:f + 1]), idx) - rec[f:f + 1] for f in range(6)]
+            diff = [near[j, f] - rec[f:f + 1] for f in range(6)]
             gain = rec[6:7] / (1.0 + diff[0] * diff[0] + diff[1] * diff[1] + diff[2] * diff[2])
             force = jnp.zeros((8, LANES), F32)
             for f in range(3):
@@ -299,11 +316,21 @@
             state = part[j] + change
             part[j] = state + jnp.where(sub < 3, TIME_STEP * pltpu.roll(state, 5, 0), 0.0)
 
+        lax.fori_loop(cx // 4, cx // 2, lap_rows, 0)
+        cell_row = cells_v[s, 0]
+        col_row = cell_row >> 7
+
+        def hot_chunk(i, _):
+            cols = lax.broadcasted_iota(jnp.int32, (chunk, n_rec), 0) + i * chunk
+            rec_hot[pl.ds(pl.multiple_of(i * chunk, chunk), chunk), :] = jnp.where(cols == col_row, 1.0, 0.0).astype(BF16)
+            return 0
+
+        lax.fori_loop(0, cx // chunk_x, hot_chunk, 0)
+
         for k in range(1, n_gy):
             src = lax.rem(b + k, n_gy)
             wait_from(ax.at[p, src], a_recv.at[p, src])
-        cell_row = cells_v[pl.ds(s, 1), :]
-        own_row = owner_v[pl.ds(s, 1), :]
+        own_row = owner_v[s, 0]
         rank_row = rank[pl.ds(s, 1), :]
         zrow = lax.broadcasted_iota(jnp.int32, (LANES, LANES), 0)
         for w in range(rec_tiles):
@@ -316,8 +343,8 @@
             hi, lo = two_parts(push)
             here = zrow == (cell_row[:, ws] & 127)
             for f in range(3):
-                b_hi[f * LANES:(f + 1) * LANES, ws] = jnp.where(here, hi[f:f + 1], 0.0).astype(BF16)
-                b_lo[f * LANES:(f + 1) * LANES, ws] = jnp.where(here, lo[f:f + 1], 0.0).astype(BF16)
+                b_both[2 * f * LANES:(2 * f + 1) * LANES, ws] = jnp.where(here, hi[f:f + 1], 0.0).astype(BF16)
+                b_both[(2 * f + 1) * LANES:(2 * f + 2) * LANES, ws] = jnp.where(here, lo[f:f + 1], 0.0).astype(BF16)
         for copy in m_copies + a_copies + [p_copy]:
             copy.wait_send()
         for there, copy, _k in halos + y_halos:
@@ -325,16 +352,13 @@
             def _(copy=copy):
                 copy.wait_send()
 
-        col_row = cell_row >> 7
-
         def add_chunk(i, _):
             x0 = i * chunk_x
-            cols = lax.broadcasted_iota(jnp.int32, (chunk, n_rec), 0) + i * chunk
-            hot = jnp.where(cols == col_row, 1.0, 0.0).astype(BF16)
+            hot = rec_hot[pl.ds(pl.multiple_of(i * chunk, chunk), chunk), :]
             base = pl.multiple_of(i * (chunk * 8), chunk * 8)
             for f in range(3):
-                fs = pl.ds(f * LANES, LANES)
-                add = dot_nt(hot, b_hi[fs, :]) + dot_nt(hot, b_lo[fs, :])
+                both = dot_nt(hot, b_both[pl.ds(2 * f * LANES, 2 * LANES), :])
+                add = both[:, :LANES] + both[:, LANES:]
                 v = V[f, pl.ds(x0, chunk_x)].reshape(chunk, LANES) + add
                 d = D[f, pl.ds(x0 + 1, chunk_x)].reshape(chunk, LANES) + TIME_STEP * v
                 V[f, pl.ds(x0, chunk_x)] = v.reshape(chunk_x, cy, LANES)
@@ -367,21 +391,26 @@
     n_nbr = bnbr.shape[2]
     dims = (n_gx, n_gy, cx, cy, steps, n_rec, n_seg, n_blocks, n_nbr)
     contact = contact_cells.reshape(1, n_seg)
-    cells = eroded.reshape(steps, n_rec)
+    cells = eroded.reshape(steps, 1, 1, n_rec)
     vm = pl.BlockSpec(memory_space=pltpu.VMEM)
     sm = pl.BlockSpec(memory_space=pltpu.SMEM)
+    anywhere = pl.BlockSpec(memory_space=pl.ANY)
     dma = pltpu.SemaphoreType.DMA
     tile = (8, LANES)
     return pl.pallas_call(
         functools.partial(kernel, dims),
         out_shape=(jax.ShapeDtypeStruct(disp.shape, F32), jax.ShapeDtypeStruct(vel.shape, F32)),
-        in_specs=[sm, sm] + [vm] * 11,
-        out_specs=(pl.BlockSpec(memory_space=pl.ANY), pl.BlockSpec(memory_space=pl.ANY)),
+        in_specs=[sm, sm] + [anywhere] * 4 + [vm] * 7,
+        out_specs=(anywhere, anywhere),
         scratch_shapes=[
             pltpu.VMEM((3, cx + 2, cy, nz), F32),
             pltpu.VMEM((3, cx, cy, nz), F32),
             pltpu.VMEM((cx, cy, nz), F32),
+            pltpu.VMEM((cx, cy, nz), F32),
             pltpu.VMEM((cx * cy, 8, nz), F32),
+            pltpu.VMEM((n_rec // LANES,) + tile, F32),
+            pltpu.VMEM((n_blocks, 6) + tile, F32),
+            pltpu.VMEM((cx * cy, n_rec), BF16),
             pltpu.VMEM((cx * cy, nz), F32),
             pltpu.VMEM((2, 3, cx, nz), F32),
             pltpu.VMEM((2, 2, 3, cx, nz), F32),
@@ -398,20 +427,19 @@
             pltpu.VMEM((n_blocks,) + tile, jnp.int32),
             pltpu.VMEM((n_blocks, n_nbr * LANES, LANES), BF16),
             pltpu.VMEM((cx * cy, n_seg), BF16),
-            pltpu.VMEM((3 * LANES, n_rec), BF16),
-            pltpu.VMEM((3 * LANES, n_rec), BF16),
-            dma((2,)),
+            pltpu.VMEM((6 * LANES, n_rec), BF16),
+            dma((2,)), dma((4,)),
             dma((2,)), dma((2, 2)),
             dma((2,)), dma((2, 2)),
             dma((n_gy,)), dma((2, n_gy)),
             dma((n_gy,)), dma((2, n_gy)),
             dma, dma((2,)),
         ],
-        compiler_params=pltpu.CompilerParams(collective_id=0, has_side_effects=True, vmem_limit_bytes=48 * 2**20),
+        compiler_params=pltpu.CompilerParams(collective_id=0, has_side_effects=True, vmem_limit_bytes=60 * 2**20),
         name="dynamics",
     )(
         cells, contact, disp, vel, stiff, mass, contact, contact_match.reshape(1, n_seg), cells,
-        owners.reshape(steps, n_rec), bpos[0, 0], bvel[0, 0], bnbr[0, 0],
+        owners.reshape(steps, 1, 1, n_rec), bpos[0, 0], bvel[0, 0], bnbr[0, 0],
     )
 
 

time: 214 us -> 122 us (0.57)
  Pallas kernels: 203 us -> 116 us
  local copies, waits for them, and re-layouts: 10.1 us -> 5.27 us
    pallas_call x1, Pallas kernels: 203 us -> 116 us  [local(): pl.pallas_call(functools.partial(kernel, dims), out_shape=(jax.ShapeDtype...]
    unnamed x17 -> x5, local copies, waits for them, and re-layouts: 10.1 us -> 5.27 us
where the time goes in v1:
time: 122 us
  Pallas kernels  116 us (95%)
  local copies, waits for them, and re-layouts  5.27 us (4%)
    pallas_call x1, Pallas kernels, local(): pl.pallas_call(functools.partial(kernel, dims), out_shape=(jax.ShapeDtype...  116 us
    unnamed x5, local copies, waits for them, and re-layouts  5.27 us

profile of v1, /device:TPU:0, one launch (start us, length us, event | category | flops | bytes accessed | tf_op | source)
XLA Modules:
  0.0 122.1 jit_solution(9653721265302088407)
XLA Ops:
  0.6 1.3 %copy_bitcast_fusion = (f32[3,1024]{1,0:T(4,128)}, f32[3,1024]{1,0:T(4,128)}) fusion(f32[1,1,3,1024]{3,1,2,0:T(1,128)} %param.20, f32[1,1,3,1024]{3,1,2,0:T(1,128)} %param.19), kind=kLoop, calls=%fused_computation | loop fusion | bytes 49152
  2.0 116.2 %dynamics.1 = (f32[3,32,32,128]{3,2,1,0:T(8,128)}, f32[3,32,32,128]{3,2,1,0:T(8,128)}) custom-call(s32[8,1,1,512]{3,2,1,0:T(1,128)} %cells_v.1, s32[1,512]{1,0:T(1,128)} %bitcast.10, f32[3,32,32,128]{3,2,1,0:T(8,128)} %disp_in.1, f32[3,32,32,128]{3,2,1,0:T(8,128)} %vel_in.1, f32[32,32,128]{2,1,0:T(8,128)} %stiff_in.1, f32[32,32,128]{2,1,0:T(8,128)} %mass_in.1, ...), custom_call_target="tpu_custom_call" | custom-call | tf_op jit(solution)/shard_map/dynamics/pallas_call | solution.py:400
  118.2 0.0 copy-start
  118.2 2.8 %copy.19 = f32[3,32,32,128]{3,2,1,0:T(8,128)} copy(f32[3,32,32,128]{3,2,1,0:T(8,128)} %get-tuple-element.6) | data formatting | bytes 3145728
  121.0 0.0 copy-done
  121.0 1.1 copy.20
Async XLA Ops:
  118.2 2.8 %copy-start = (f32[3,32,32,128]{3,2,1,0:T(8,128)S(1)}, f32[3,32,32,128]{3,2,1,0:T(8,128)}, u32[]{:S(2)}) copy-start(f32[3,32,32,128]{3,2,1,0:T(8,128)} %get-tuple-element.7) | copy-start | bytes 4718596

commit v2 on v1

--- a/solution.py
+++ b/solution.py
@@ -38,7 +38,7 @@
     dims,
     cells_s, contact_s, disp_in, vel_in, stiff_in, mass_in, contact_v, match_v, cells_v, owner_v, bpos, bvel, bnbr,
     disp_out, vel_out,
-    D, V, A, M, G, recs_buf, near, rec_hot, top_add, ye, yh, xh, msg, rx, ans, ax, seg, ps, inv, rank, part, nbr, nbr_hot, seg_hot, b_both,
+    D, V, A, M, G, recs_buf, seg_pre, push_buf, near, match_hot, cell_col, top_add, ye, yh, xh, msg, rx, ans, ax, seg, ps, inv, rank, part, nbr, nbr_hot, seg_hot, b_both,
     out_sem, in_sem, ye_send, yh_recv, xe_send, xh_recv, m_send, m_recv, a_send, a_recv, p_send, p_recv,
 ):
     n_gx, n_gy, cx, cy, steps, n_rec, n_seg, n_blocks, n_nbr = dims
@@ -66,6 +66,7 @@
         load.start()
     yh[...] = jnp.zeros_like(yh)
     xh[...] = jnp.zeros_like(xh)
+    push_buf[...] = jnp.zeros_like(push_buf)
 
 
     tri = jnp.where(
@@ -85,6 +86,10 @@
         q_hot = jnp.where(lax.broadcasted_iota(jnp.int32, (LANES, n_rec), 0) == rk, 1.0, 0.0).astype(BF16)
         both = dot_nt(jnp.concatenate([lo, hi], axis=0).astype(BF16), q_hot)
         inv[s] = (both[:n_gy] + 128.0 * both[n_gy:]).astype(jnp.int32) - 1
+        cell_row = cells_v[s, 0].astype(F32)
+        for w in range(rec_tiles):
+            ws = slice(w * LANES, (w + 1) * LANES)
+            cell_col[s, ws, :] = jnp.broadcast_to(cell_row[:, ws], (LANES, LANES)).T
         return 0
 
     lax.fori_loop(0, steps, init_step, 0)
@@ -148,8 +153,66 @@
     def remote(src, dst, send, recv, to):
         return pltpu.make_async_remote_copy(src_ref=src, dst_ref=dst, send_sem=send, recv_sem=recv, device_id=to, device_id_type=MESH)
 
+    def read_records(s):
+        def read_rec(w, _):
+            acc = jnp.zeros((8, LANES), F32)
+            for t in range(LANES):
+                cell = cells_s[s, 0, 0, w * LANES + t]
+                acc = jnp.where(lane == t, take_lanes(G[cell >> 7], jnp.full((8, LANES), cell & 127, jnp.int32)), acc)
+            recs_buf[w] = acc
+            return 0
+
+        lax.fori_loop(0, rec_tiles, read_rec, 0)
+
+    def read_segments():
+        def read_seg(w, _):
+            acc = jnp.zeros((8, LANES), F32)
+            for t in range(LANES):
+                acc = jnp.where(lane == t, pltpu.roll(G[contact_s[0, w * LANES + t]], (t + 1) % LANES, 1), acc)
+            seg_pre[w] = acc
+            return 0
+
+        lax.fori_loop(0, seg_tiles, read_seg, 0)
+
+    def add_forces(s):
+        cell_row = cells_v[s, 0]
+        col_row = cell_row >> 7
+        zrow = lax.broadcasted_iota(jnp.int32, (LANES, LANES), 0)
+        for w in range(rec_tiles):
+            ws = slice(w * LANES, (w + 1) * LANES)
+            here = zrow == (cell_row[:, ws] & 127)
+            for f in range(3):
+                for q in range(2):
+                    b_both[(2 * f + q) * LANES:(2 * f + q + 1) * LANES, ws] = jnp.where(
+                        here, push_buf[q, w, f:f + 1, :], 0.0
+                    ).astype(BF16)
+
+        def add_chunk(i, _):
+            x0 = i * chunk_x
+            cols = lax.broadcasted_iota(jnp.int32, (chunk, n_rec), 0) + i * chunk
+            hot = jnp.where(cols == col_row, 1.0, 0.0).astype(BF16)
+            for f in range(3):
+                both = dot_nt(hot, b_both[pl.ds(2 * f * LANES, 2 * LANES), :])
+                add = both[:, :LANES] + both[:, LANES:]
+                v = V[f, pl.ds(x0, chunk_x)].reshape(chunk, LANES) + add
+                d = D[f, pl.ds(x0 + 1, chunk_x)].reshape(chunk, LANES) + TIME_STEP * v
+                V[f, pl.ds(x0, chunk_x)] = v.reshape(chunk_x, cy, LANES)
+                D[f, pl.ds(x0 + 1, chunk_x)] = d.reshape(chunk_x, cy, LANES)
+                for xx in range(chunk_x):
+                    ye[0, f, pl.ds(x0 + xx, 1), :] = d[xx * cy:xx * cy + 1]
+                    ye[1, f, pl.ds(x0 + xx, 1), :] = d[xx * cy + cy - 1:xx * cy + cy]
+            return 0
+
+        lax.fori_loop(0, cx // chunk_x, add_chunk, 0)
+
+    read_records(0)
+    read_segments()
+    for w in range(seg_tiles):
+        seg[w] = seg_pre[w]
+
     def step(s, _):
         p = lax.rem(s, 2)
+        after = jnp.minimum(s + 1, steps - 1)
         halos = (
             (a > 0, remote(D.at[:, 1], xh.at[p, 1], xe_send.at[0], xh_recv.at[p, 1], (a - 1, b)), 0),
             (a < n_gx - 1, remote(D.at[:, cx], xh.at[p, 0], xe_send.at[1], xh_recv.at[p, 0], (a + 1, b)), 1),
@@ -159,20 +222,9 @@
             (b < n_gy - 1, remote(ye.at[1], yh.at[p, 0], ye_send.at[1], yh_recv.at[p, 0], (a, b + 1)), 1),
         )
 
-        for there, copy, _k in halos + y_halos:
-            @pl.when(there)
-            def _(copy=copy):
-                copy.start()
-
-        def read_rec(w, _):
-            acc = jnp.zeros((8, LANES), F32)
-            for t in range(LANES):
-                cell = cells_s[s, 0, 0, w * LANES + t]
-                acc = jnp.where(lane == t, take_lanes(G[cell >> 7], jnp.full((8, LANES), cell & 127, jnp.int32)), acc)
-            recs_buf[w] = acc
-            return 0
-
-        lax.fori_loop(0, rec_tiles, read_rec, 0)
+        def wait_from(dst, recv):
+            pltpu.make_async_copy(dst, dst, recv).wait()
+
         recs = [recs_buf[w] for w in range(rec_tiles)]
         for o in range(n_gy):
             idx = rows8(inv[s, o:o + 1, :])
@@ -186,38 +238,35 @@
             o = lax.rem(b + k, n_gy)
             m_copies.append(remote(msg.at[o], rx.at[p, b], m_send.at[k], m_recv.at[p, b], (a, o)))
             m_copies[-1].start()
-        def read_seg(w, _):
-            acc = jnp.zeros((8, LANES), F32)
-            for t in range(LANES):
-                acc = jnp.where(lane == t, pltpu.roll(G[contact_s[0, w * LANES + t]], (t + 1) % LANES, 1), acc)
-            seg[w] = acc
-            return 0
-
-        lax.fori_loop(0, seg_tiles, read_seg, 0)
         p_copy = remote(seg, ps.at[p], p_send, p_recv.at[p], (mate, b))
         p_copy.start()
 
-        def wait_from(dst, recv):
-            pltpu.make_async_copy(dst, dst, recv).wait()
-
-        @pl.when(a > 0)
+        @pl.when(s > 0)
         def _():
-            wait_from(xh.at[p, 0], xh_recv.at[p, 0])
-
-        @pl.when(a < n_gx - 1)
-        def _():
-            wait_from(xh.at[p, 1], xh_recv.at[p, 1])
-
-        @pl.when(b > 0)
-        def _():
-            wait_from(yh.at[p, 0], yh_recv.at[p, 0])
-
-        @pl.when(b < n_gy - 1)
-        def _():
-            wait_from(yh.at[p, 1], yh_recv.at[p, 1])
-
-        D[:, 0] = xh[p, 0]
-        D[:, cx + 1] = xh[p, 1]
+            add_forces(s - 1)
+
+        for there, copy, _k in halos + y_halos:
+            @pl.when(there)
+            def _(copy=copy):
+                copy.start()
+
+        goal = jnp.concatenate([cells_v[after, 0], contact_v[...] * LANES + (LANES - 1)], axis=1).astype(F32)
+
+        def match_tile(w, _):
+            at = pl.ds(pl.multiple_of(w * LANES, LANES), LANES)
+            col = cell_col[s, at, :]
+            for t in range(rec_tiles + seg_tiles):
+                ts = slice(t * LANES, (t + 1) * LANES)
+                match_hot[at, ts] = jnp.where(col == goal[:, ts], 1.0, 0.0).astype(BF16)
+            return 0
+
+        lax.fori_loop(0, rec_tiles, match_tile, 0)
+        for j in range(n_blocks):
+            state = part[j]
+            idx = nbr[j]
+            for f in range(6):
+                near[j, f] = take_lanes(rows8(state[f:f + 1]), idx)
+
         wait_from(ps.at[p], p_recv.at[p])
         c_parts = [[], []]
         for w in range(seg_tiles):
@@ -231,16 +280,37 @@
             c_parts[0].append(hi)
             c_parts[1].append(lo)
         zero_rows = jnp.zeros((LANES - 8, n_seg), F32)
-        c_mats = [jnp.concatenate([zero_rows, jnp.concatenate(part_, axis=1)], axis=0).astype(BF16) for part_ in c_parts]
+        c_mat = jnp.concatenate(
+            [zero_rows, jnp.concatenate(c_parts[0], axis=1), zero_rows, jnp.concatenate(c_parts[1], axis=1)], axis=0
+        ).astype(BF16)
 
         def top_chunk(i, _):
             at = pl.ds(pl.multiple_of(i * chunk, chunk), chunk)
             hot = seg_hot[at, :]
-            top_add[at, :] = dot_nt(hot, c_mats[0]) + dot_nt(hot, c_mats[1])
+            both = dot_nt(hot, c_mat)
+            top_add[at, :] = both[:, :LANES] + both[:, LANES:]
             return 0
 
         lax.fori_loop(0, cx // chunk_x, top_chunk, 0)
 
+        @pl.when(a > 0)
+        def _():
+            wait_from(xh.at[p, 0], xh_recv.at[p, 0])
+
+        @pl.when(a < n_gx - 1)
+        def _():
+            wait_from(xh.at[p, 1], xh_recv.at[p, 1])
+
+        @pl.when(b > 0)
+        def _():
+            wait_from(yh.at[p, 0], yh_recv.at[p, 0])
+
+        @pl.when(b < n_gy - 1)
+        def _():
+            wait_from(yh.at[p, 1], yh_recv.at[p, 1])
+
+        D[:, 0] = xh[p, 0]
+        D[:, cx + 1] = xh[p, 1]
         row_i = lax.broadcasted_iota(jnp.int32, (cy, LANES), 0)
         lane_i = lax.broadcasted_iota(jnp.int32, (cy, LANES), 1)
 
@@ -255,19 +325,18 @@
                 lap += jnp.where(lane_i == 0, 0.0, pltpu.roll(c, 1, 1))
                 lap += jnp.where(lane_i == LANES - 1, 0.0, pltpu.roll(c, LANES - 1, 1))
                 push = jnp.where(lane_i == LANES - 1, pltpu.roll(top, 2 - f, 1) if f < 2 else top, 0.0)
-                V[f, x] = V[f, x] + scale * lap + push
+                v = V[f, x] + scale * lap + push
+                V[f, x] = v
+                base = pl.multiple_of(x * (cy * 8), cy * 8)
+                flat[pl.ds(base + f, cy, stride=8), :] = c + TIME_STEP * v
+                flat[pl.ds(base + 3 + f, cy, stride=8), :] = v
 
         def lap_rows(i, _):
             lap_row(2 * i)
             lap_row(2 * i + 1)
             return 0
 
-        lax.fori_loop(0, cx // 4, lap_rows, 0)
-        for j in range(n_blocks):
-            state = part[j]
-            idx = nbr[j]
-            for f in range(6):
-                near[j, f] = take_lanes(rows8(state[f:f + 1]), idx)
+        lax.fori_loop(0, cx // 8, lap_rows, 0)
 
         for k in range(1, n_gy):
             src = lax.rem(b + k, n_gy)
@@ -316,64 +385,44 @@
             state = part[j] + change
             part[j] = state + jnp.where(sub < 3, TIME_STEP * pltpu.roll(state, 5, 0), 0.0)
 
-        lax.fori_loop(cx // 4, cx // 2, lap_rows, 0)
-        cell_row = cells_v[s, 0]
-        col_row = cell_row >> 7
-
-        def hot_chunk(i, _):
-            cols = lax.broadcasted_iota(jnp.int32, (chunk, n_rec), 0) + i * chunk
-            rec_hot[pl.ds(pl.multiple_of(i * chunk, chunk), chunk), :] = jnp.where(cols == col_row, 1.0, 0.0).astype(BF16)
-            return 0
-
-        lax.fori_loop(0, cx // chunk_x, hot_chunk, 0)
+        lax.fori_loop(cx // 8, cx // 2, lap_rows, 0)
+        masses = [recs_buf[w, 6:7, :] for w in range(rec_tiles)]
+        read_records(after)
+        read_segments()
 
         for k in range(1, n_gy):
             src = lax.rem(b + k, n_gy)
             wait_from(ax.at[p, src], a_recv.at[p, src])
         own_row = owner_v[s, 0]
         rank_row = rank[pl.ds(s, 1), :]
-        zrow = lax.broadcasted_iota(jnp.int32, (LANES, LANES), 0)
+        rows = []
         for w in range(rec_tiles):
             ws = slice(w * LANES, (w + 1) * LANES)
             own8, rank8 = rows8(own_row[:, ws]), rows8(rank_row[:, ws])
             force = jnp.zeros((8, LANES), F32)
             for o in range(n_gy):
                 force = jnp.where(own8 == o, take_lanes(ax[p, o], rank8), force)
-            push = TIME_STEP * force / recs[w][6:7]
-            hi, lo = two_parts(push)
-            here = zrow == (cell_row[:, ws] & 127)
-            for f in range(3):
-                b_both[2 * f * LANES:(2 * f + 1) * LANES, ws] = jnp.where(here, hi[f:f + 1], 0.0).astype(BF16)
-                b_both[(2 * f + 1) * LANES:(2 * f + 2) * LANES, ws] = jnp.where(here, lo[f:f + 1], 0.0).astype(BF16)
+            hi, lo = two_parts(TIME_STEP * force / masses[w])
+            push_buf[0, w] = hi
+            push_buf[1, w] = lo
+            rows.append(jnp.concatenate([hi, lo], axis=0))
+        both = jnp.dot(jnp.concatenate(rows, axis=1).astype(BF16), match_hot[...], preferred_element_type=F32)
+        more = both[:8] + both[8:]
+        more = TIME_STEP * more + pltpu.roll(more, 3, 0)
         for copy in m_copies + a_copies + [p_copy]:
             copy.wait_send()
         for there, copy, _k in halos + y_halos:
             @pl.when(there)
             def _(copy=copy):
                 copy.wait_send()
-
-        def add_chunk(i, _):
-            x0 = i * chunk_x
-            hot = rec_hot[pl.ds(pl.multiple_of(i * chunk, chunk), chunk), :]
-            base = pl.multiple_of(i * (chunk * 8), chunk * 8)
-            for f in range(3):
-                both = dot_nt(hot, b_both[pl.ds(2 * f * LANES, 2 * LANES), :])
-                add = both[:, :LANES] + both[:, LANES:]
-                v = V[f, pl.ds(x0, chunk_x)].reshape(chunk, LANES) + add
-                d = D[f, pl.ds(x0 + 1, chunk_x)].reshape(chunk, LANES) + TIME_STEP * v
-                V[f, pl.ds(x0, chunk_x)] = v.reshape(chunk_x, cy, LANES)
-                D[f, pl.ds(x0 + 1, chunk_x)] = d.reshape(chunk_x, cy, LANES)
-                flat[pl.ds(base + f, chunk, stride=8), :] = d
-                flat[pl.ds(base + 3 + f, chunk, stride=8), :] = v
-                for xx in range(chunk_x):
-                    ye[0, f, pl.ds(x0 + xx, 1), :] = d[xx * cy:xx * cy + 1]
-                    ye[1, f, pl.ds(x0 + xx, 1), :] = d[xx * cy + cy - 1:xx * cy + cy]
-            return 0
-
-        lax.fori_loop(0, cx // chunk_x, add_chunk, 0)
+        for w in range(rec_tiles):
+            recs_buf[w] = recs_buf[w] + more[:, w * LANES:(w + 1) * LANES]
+        for w in range(seg_tiles):
+            seg[w] = seg_pre[w] + more[:, n_rec + w * LANES:n_rec + (w + 1) * LANES]
         return 0
 
     lax.fori_loop(0, steps, step, 0)
+    add_forces(steps - 1)
     out_d = pltpu.make_async_copy(D.at[:, pl.ds(1, cx)], disp_out, out_sem.at[0])
     out_v = pltpu.make_async_copy(V, vel_out, out_sem.at[1])
     out_d.start()
@@ -409,8 +458,11 @@
             pltpu.VMEM((cx, cy, nz), F32),
             pltpu.VMEM((cx * cy, 8, nz), F32),
             pltpu.VMEM((n_rec // LANES,) + tile, F32),
+            pltpu.VMEM((n_seg // LANES,) + tile, F32),
+            pltpu.VMEM((2, n_rec // LANES) + tile, F32),
             pltpu.VMEM((n_blocks, 6) + tile, F32),
-            pltpu.VMEM((cx * cy, n_rec), BF16),
+            pltpu.VMEM((n_rec, n_rec + n_seg), BF16),
+            pltpu.VMEM((steps, n_rec, LANES), F32),
             pltpu.VMEM((cx * cy, nz), F32),
             pltpu.VMEM((2, 3, cx, nz), F32),
             pltpu.VMEM((2, 2, 3, cx, nz), F32),

time: 122 us -> 121 us (level)
  no operation moved by 1% of the time
where the time goes in v2:
time: 121 us
  Pallas kernels  115 us (95%)
  local copies, waits for them, and re-layouts  5.27 us (4%)
    pallas_call x1, Pallas kernels, local(): pl.pallas_call(functools.partial(kernel, dims), out_shape=(jax.ShapeDtype...  115 us
    unnamed x5, local copies, waits for them, and re-layouts  5.27 us

profile of v2, /device:TPU:0, one launch (start us, length us, event | category | flops | bytes accessed | tf_op | source)
XLA Modules:
  0.0 121.0 jit_solution(8010513254310377663)
XLA Ops:
  0.6 1.3 %copy_bitcast_fusion = (f32[3,1024]{1,0:T(4,128)}, f32[3,1024]{1,0:T(4,128)}) fusion(f32[1,1,3,1024]{3,1,2,0:T(1,128)} %param.20, f32[1,1,3,1024]{3,1,2,0:T(1,128)} %param.19), kind=kLoop, calls=%fused_computation | loop fusion | bytes 49152
  2.0 115.1 %dynamics.1 = (f32[3,32,32,128]{3,2,1,0:T(8,128)}, f32[3,32,32,128]{3,2,1,0:T(8,128)}) custom-call(s32[8,1,1,512]{3,2,1,0:T(1,128)} %cells_v.1, s32[1,512]{1,0:T(1,128)} %bitcast.10, f32[3,32,32,128]{3,2,1,0:T(8,128)} %disp_in.1, f32[3,32,32,128]{3,2,1,0:T(8,128)} %vel_in.1, f32[32,32,128]{2,1,0:T(8,128)} %stiff_in.1, f32[32,32,128]{2,1,0:T(8,128)} %mass_in.1, ...), custom_call_target="tpu_custom_call" | custom-call | tf_op jit(solution)/shard_map/dynamics/pallas_call | solution.py:449
  117.1 0.0 copy-start
  117.1 2.8 %copy.19 = f32[3,32,32,128]{3,2,1,0:T(8,128)} copy(f32[3,32,32,128]{3,2,1,0:T(8,128)} %get-tuple-element.6) | data formatting | bytes 3145728
  119.9 0.0 copy-done
  119.9 1.1 copy.20
Async XLA Ops:
  117.1 2.8 %copy-start = (f32[3,32,32,128]{3,2,1,0:T(8,128)S(1)}, f32[3,32,32,128]{3,2,1,0:T(8,128)}, u32[]{:S(2)}) copy-start(f32[3,32,32,128]{3,2,1,0:T(8,128)} %get-tuple-element.7) | copy-start | bytes 4718596

commit v3 on v2

--- a/solution.py
+++ b/solution.py
@@ -55,9 +55,10 @@
     sub = lax.broadcasted_iota(jnp.int32, (8, LANES), 0)
 
     flat = G.reshape(n_cols * 8, LANES)
+    core = pl.ds(8, cy)
 
     loads = [
-        pltpu.make_async_copy(disp_in, D.at[:, pl.ds(1, cx)], in_sem.at[0]),
+        pltpu.make_async_copy(disp_in, D.at[:, pl.ds(1, cx), core], in_sem.at[0]),
         pltpu.make_async_copy(vel_in, V, in_sem.at[1]),
         pltpu.make_async_copy(stiff_in, A, in_sem.at[2]),
         pltpu.make_async_copy(mass_in, M, in_sem.at[3]),
@@ -105,7 +106,7 @@
         new = lax.rem(old, n_gy) * group + old // n_gy
         nbr[j] = new
         for k in range(n_nbr):
-            nbr_hot[j, pl.ds(k * LANES, LANES), :] = jnp.where(nrow == new[k:k + 1], 1.0, 0.0).astype(BF16)
+            nbr_hot[j, :, k * LANES:(k + 1) * LANES] = jnp.where(nrow == new[k:k + 1], 1.0, 0.0).T.astype(BF16)
         return 0
 
     lax.fori_loop(0, n_blocks, init_block, 0)
@@ -120,7 +121,7 @@
         A[xs] = TIME_STEP * A[xs] / M[xs]
         base = pl.multiple_of(i * (chunk * 8), chunk * 8)
         for f in range(3):
-            d = D[f, pl.ds(x0 + 1, chunk_x)]
+            d = D[f, pl.ds(x0 + 1, chunk_x), core]
             v = V[f, xs]
             flat[pl.ds(base + f, chunk, stride=8), :] = d.reshape(chunk, LANES)
             flat[pl.ds(base + 3 + f, chunk, stride=8), :] = v.reshape(chunk, LANES)
@@ -187,23 +188,26 @@
                         here, push_buf[q, w, f:f + 1, :], 0.0
                     ).astype(BF16)
 
+        add_x = cx // 2
+        add_n = add_x * cy
+
         def add_chunk(i, _):
-            x0 = i * chunk_x
-            cols = lax.broadcasted_iota(jnp.int32, (chunk, n_rec), 0) + i * chunk
+            x0 = i * add_x
+            cols = lax.broadcasted_iota(jnp.int32, (add_n, n_rec), 0) + i * add_n
             hot = jnp.where(cols == col_row, 1.0, 0.0).astype(BF16)
             for f in range(3):
                 both = dot_nt(hot, b_both[pl.ds(2 * f * LANES, 2 * LANES), :])
                 add = both[:, :LANES] + both[:, LANES:]
-                v = V[f, pl.ds(x0, chunk_x)].reshape(chunk, LANES) + add
-                d = D[f, pl.ds(x0 + 1, chunk_x)].reshape(chunk, LANES) + TIME_STEP * v
-                V[f, pl.ds(x0, chunk_x)] = v.reshape(chunk_x, cy, LANES)
-                D[f, pl.ds(x0 + 1, chunk_x)] = d.reshape(chunk_x, cy, LANES)
-                for xx in range(chunk_x):
+                v = V[f, pl.ds(x0, add_x)].reshape(add_n, LANES) + add
+                d = D[f, pl.ds(x0 + 1, add_x), core].reshape(add_n, LANES) + TIME_STEP * v
+                V[f, pl.ds(x0, add_x)] = v.reshape(add_x, cy, LANES)
+                D[f, pl.ds(x0 + 1, add_x), core] = d.reshape(add_x, cy, LANES)
+                for xx in range(add_x):
                     ye[0, f, pl.ds(x0 + xx, 1), :] = d[xx * cy:xx * cy + 1]
                     ye[1, f, pl.ds(x0 + xx, 1), :] = d[xx * cy + cy - 1:xx * cy + cy]
             return 0
 
-        lax.fori_loop(0, cx // chunk_x, add_chunk, 0)
+        lax.fori_loop(0, cx // add_x, add_chunk, 0)
 
     read_records(0)
     read_segments()
@@ -214,8 +218,8 @@
         p = lax.rem(s, 2)
         after = jnp.minimum(s + 1, steps - 1)
         halos = (
-            (a > 0, remote(D.at[:, 1], xh.at[p, 1], xe_send.at[0], xh_recv.at[p, 1], (a - 1, b)), 0),
-            (a < n_gx - 1, remote(D.at[:, cx], xh.at[p, 0], xe_send.at[1], xh_recv.at[p, 0], (a + 1, b)), 1),
+            (a > 0, remote(D.at[:, 1, core], xh.at[p, 1], xe_send.at[0], xh_recv.at[p, 1], (a - 1, b)), 0),
+            (a < n_gx - 1, remote(D.at[:, cx, core], xh.at[p, 0], xe_send.at[1], xh_recv.at[p, 0], (a + 1, b)), 1),
         )
         y_halos = (
             (b > 0, remote(ye.at[0], yh.at[p, 1], ye_send.at[0], yh_recv.at[p, 1], (a, b - 1)), 0),
@@ -309,19 +313,28 @@
         def _():
             wait_from(yh.at[p, 1], yh_recv.at[p, 1])
 
-        D[:, 0] = xh[p, 0]
-        D[:, cx + 1] = xh[p, 1]
-        row_i = lax.broadcasted_iota(jnp.int32, (cy, LANES), 0)
+        D[:, 0, core] = xh[p, 0]
+        D[:, cx + 1, core] = xh[p, 1]
+
+        def y_rows(i, _):
+            for u in range(8):
+                x = i * 8 + u
+                for f in range(3):
+                    D[f, x + 1, pl.ds(7, 1), :] = yh[p, 0, f, pl.ds(x, 1), :]
+                    D[f, x + 1, pl.ds(8 + cy, 1), :] = yh[p, 1, f, pl.ds(x, 1), :]
+            return 0
+
+        lax.fori_loop(0, cx // 8, y_rows, 0)
+
         lane_i = lax.broadcasted_iota(jnp.int32, (cy, LANES), 1)
 
         def lap_row(x):
             top = top_add[pl.ds(pl.multiple_of(x * cy, cy), cy), :]
             scale = A[x]
             for f in range(3):
-                c = D[f, x + 1]
-                lap = D[f, x] + D[f, x + 2] - 6.0 * c
-                lap += jnp.where(row_i == 0, yh[p, 0, f, pl.ds(x, 1), :], pltpu.roll(c, 1, 0))
-                lap += jnp.where(row_i == cy - 1, yh[p, 1, f, pl.ds(x, 1), :], pltpu.roll(c, cy - 1, 0))
+                c = D[f, x + 1, core]
+                lap = D[f, x, core] + D[f, x + 2, core] - 6.0 * c
+                lap += D[f, x + 1, pl.ds(7, cy)] + D[f, x + 1, pl.ds(9, cy)]
                 lap += jnp.where(lane_i == 0, 0.0, pltpu.roll(c, 1, 1))
                 lap += jnp.where(lane_i == LANES - 1, 0.0, pltpu.roll(c, LANES - 1, 1))
                 push = jnp.where(lane_i == LANES - 1, pltpu.roll(top, 2 - f, 1) if f < 2 else top, 0.0)
@@ -332,11 +345,11 @@
                 flat[pl.ds(base + 3 + f, cy, stride=8), :] = v
 
         def lap_rows(i, _):
-            lap_row(2 * i)
-            lap_row(2 * i + 1)
-            return 0
-
-        lax.fori_loop(0, cx // 8, lap_rows, 0)
+            for u in range(4):
+                lap_row(4 * i + u)
+            return 0
+
+        lax.fori_loop(0, cx // 16, lap_rows, 0)
 
         for k in range(1, n_gy):
             src = lax.rem(b + k, n_gy)
@@ -373,7 +386,7 @@
         for j in range(n_blocks):
             parts = [two_parts(springs[3 * j + f]) for f in range(3)]
             lhs = jnp.concatenate([q[0] for q in parts] + [q[1] for q in parts], axis=0).astype(BF16)
-            wide = dot_nt(lhs, nbr_hot[j])
+            wide = jnp.dot(lhs, nbr_hot[j], preferred_element_type=F32)
             change = jnp.zeros((8, LANES), F32)
             for f in range(3):
                 acc = jnp.zeros((8, LANES), F32)
@@ -385,7 +398,7 @@
             state = part[j] + change
             part[j] = state + jnp.where(sub < 3, TIME_STEP * pltpu.roll(state, 5, 0), 0.0)
 
-        lax.fori_loop(cx // 8, cx // 2, lap_rows, 0)
+        lax.fori_loop(cx // 16, cx // 4, lap_rows, 0)
         masses = [recs_buf[w, 6:7, :] for w in range(rec_tiles)]
         read_records(after)
         read_segments()
@@ -423,7 +436,7 @@
 
     lax.fori_loop(0, steps, step, 0)
     add_forces(steps - 1)
-    out_d = pltpu.make_async_copy(D.at[:, pl.ds(1, cx)], disp_out, out_sem.at[0])
+    out_d = pltpu.make_async_copy(D.at[:, pl.ds(1, cx), core], disp_out, out_sem.at[0])
     out_v = pltpu.make_async_copy(V, vel_out, out_sem.at[1])
     out_d.start()
     out_v.start()
@@ -452,7 +465,7 @@
         in_specs=[sm, sm] + [anywhere] * 4 + [vm] * 7,
         out_specs=(anywhere, anywhere),
         scratch_shapes=[
-            pltpu.VMEM((3, cx + 2, cy, nz), F32),
+            pltpu.VMEM((3, cx + 2, cy + 16, nz), F32),
             pltpu.VMEM((3, cx, cy, nz), F32),
             pltpu.VMEM((cx, cy, nz), F32),
             pltpu.VMEM((cx, cy, nz), F32),
@@ -477,7 +490,7 @@
             pltpu.VMEM((steps, n_rec), jnp.int32),
             pltpu.VMEM((n_blocks,) + tile, F32),
             pltpu.VMEM((n_blocks,) + tile, jnp.int32),
-            pltpu.VMEM((n_blocks, n_nbr * LANES, LANES), BF16),
+            pltpu.VMEM((n_blocks, LANES, n_nbr * LANES), BF16),
             pltpu.VMEM((cx * cy, n_seg), BF16),
             pltpu.VMEM((6 * LANES, n_rec), BF16),
             dma((2,)), dma((4,)),

time: 121 us -> 111 us (0.917)
  Pallas kernels: 115 us -> 105 us
    pallas_call x1, Pallas kernels: 115 us -> 105 us  [local(): pl.pallas_call(functools.partial(kernel, dims), out_shape=(jax.ShapeDtype...]
where the time goes in v3:
time: 111 us
  Pallas kernels  105 us (95%)
  local copies, waits for them, and re-layouts  5.27 us (5%)
    pallas_call x1, Pallas kernels, local(): pl.pallas_call(functools.partial(kernel, dims), out_shape=(jax.ShapeDtype...  105 us
    unnamed x5, local copies, waits for them, and re-layouts  5.27 us

profile of v3, /device:TPU:0, one launch (start us, length us, event | category | flops | bytes accessed | tf_op | source)
XLA Modules:
  0.0 111.0 jit_solution(2839401297251143113)
XLA Ops:
  0.6 1.3 %copy_bitcast_fusion = (f32[3,1024]{1,0:T(4,128)}, f32[3,1024]{1,0:T(4,128)}) fusion(f32[1,1,3,1024]{3,1,2,0:T(1,128)} %param.20, f32[1,1,3,1024]{3,1,2,0:T(1,128)} %param.19), kind=kLoop, calls=%fused_computation | loop fusion | bytes 49152
  2.0 105.1 %dynamics.1 = (f32[3,32,32,128]{3,2,1,0:T(8,128)}, f32[3,32,32,128]{3,2,1,0:T(8,128)}) custom-call(s32[8,1,1,512]{3,2,1,0:T(1,128)} %cells_v.1, s32[1,512]{1,0:T(1,128)} %bitcast.10, f32[3,32,32,128]{3,2,1,0:T(8,128)} %disp_in.1, f32[3,32,32,128]{3,2,1,0:T(8,128)} %vel_in.1, f32[32,32,128]{2,1,0:T(8,128)} %stiff_in.1, f32[32,32,128]{2,1,0:T(8,128)} %mass_in.1, ...), custom_call_target="tpu_custom_call" | custom-call | tf_op jit(solution)/shard_map/dynamics/pallas_call | solution.py:462
  107.1 0.0 copy-start
  107.1 2.8 %copy.19 = f32[3,32,32,128]{3,2,1,0:T(8,128)} copy(f32[3,32,32,128]{3,2,1,0:T(8,128)} %get-tuple-element.6) | data formatting | bytes 3145728
  109.9 0.0 copy-done
  109.9 1.1 %copy.20 = f32[3,32,32,128]{3,2,1,0:T(8,128)} copy(f32[3,32,32,128]{3,2,1,0:T(8,128)S(1)} %copy-done) | data formatting | bytes 3145728
Async XLA Ops:
  107.1 2.8 %copy-start = (f32[3,32,32,128]{3,2,1,0:T(8,128)S(1)}, f32[3,32,32,128]{3,2,1,0:T(8,128)}, u32[]{:S(2)}) copy-start(f32[3,32,32,128]{3,2,1,0:T(8,128)} %get-tuple-element.7) | copy-start | bytes 4718596

commit v4 on v3

--- a/solution.py
+++ b/solution.py
@@ -100,9 +100,9 @@
 
     def init_block(j, _):
         at = pl.ds(pl.multiple_of(j * LANES, LANES), LANES)
-        rows = jnp.concatenate([bpos[:, at], bvel[:, at], jnp.zeros((2, LANES), F32)], axis=0)
+        rows = jnp.concatenate([bpos[f, 0, :, at] for f in range(3)] + [bvel[f, 0, :, at] for f in range(3)] + [jnp.zeros((2, LANES), F32)], axis=0)
         part[j] = take_lanes(rows, perm)
-        old = take_lanes(bnbr[:, at], perm)
+        old = take_lanes(bnbr[0, 0, :, at], perm)
         new = lax.rem(old, n_gy) * group + old // n_gy
         nbr[j] = new
         for k in range(n_nbr):
@@ -288,14 +288,16 @@
             [zero_rows, jnp.concatenate(c_parts[0], axis=1), zero_rows, jnp.concatenate(c_parts[1], axis=1)], axis=0
         ).astype(BF16)
 
+        half = n_cols // 2
+
         def top_chunk(i, _):
-            at = pl.ds(pl.multiple_of(i * chunk, chunk), chunk)
+            at = pl.ds(pl.multiple_of(i * half, half), half)
             hot = seg_hot[at, :]
             both = dot_nt(hot, c_mat)
             top_add[at, :] = both[:, :LANES] + both[:, LANES:]
             return 0
 
-        lax.fori_loop(0, cx // chunk_x, top_chunk, 0)
+        lax.fori_loop(0, n_cols // half, top_chunk, 0)
 
         @pl.when(a > 0)
         def _():
@@ -400,8 +402,12 @@
 
         lax.fori_loop(cx // 16, cx // 4, lap_rows, 0)
         masses = [recs_buf[w, 6:7, :] for w in range(rec_tiles)]
-        read_records(after)
-        read_segments()
+
+        @pl.when(s < steps - 1)
+        def _():
+            read_records(after)
+            read_segments()
+
 
         for k in range(1, n_gy):
             src = lax.rem(b + k, n_gy)
@@ -504,7 +510,7 @@
         name="dynamics",
     )(
         cells, contact, disp, vel, stiff, mass, contact, contact_match.reshape(1, n_seg), cells,
-        owners.reshape(steps, 1, 1, n_rec), bpos[0, 0], bvel[0, 0], bnbr[0, 0],
+        owners.reshape(steps, 1, 1, n_rec), bpos.transpose(2, 0, 1, 3), bvel.transpose(2, 0, 1, 3), bnbr,
     )
 
 

time: 111 us -> 110 us (level)
  local copies, waits for them, and re-layouts: 5.27 us -> 3.93 us
    unnamed x5 -> x4, local copies, waits for them, and re-layouts: 5.27 us -> 3.93 us
where the time goes in v4:
time: 110 us
  Pallas kernels  105 us (95%)
  local copies, waits for them, and re-layouts  3.93 us (4%)
    pallas_call x1, Pallas kernels, local(): pl.pallas_call(functools.partial(kernel, dims), out_shape=(jax.ShapeDtype...  105 us
    unnamed x4, local copies, waits for them, and re-layouts  3.93 us

profile of v4, /device:TPU:0, one launch (start us, length us, event | category | flops | bytes accessed | tf_op | source)
XLA Modules:
  0.0 109.6 jit_solution(2766686655475896509)
XLA Ops:
  0.6 105.1 %dynamics.1 = (f32[3,32,32,128]{3,2,1,0:T(8,128)}, f32[3,32,32,128]{3,2,1,0:T(8,128)}) custom-call(s32[8,1,1,512]{3,2,1,0:T(1,128)} %cells_v.1, s32[1,512]{1,0:T(1,128)} %bitcast.8, f32[3,32,32,128]{3,2,1,0:T(8,128)} %disp_in.1, f32[3,32,32,128]{3,2,1,0:T(8,128)} %vel_in.1, f32[32,32,128]{2,1,0:T(8,128)} %stiff_in.1, f32[32,32,128]{2,1,0:T(8,128)} %mass_in.1, ...), custom_call_target="tpu_custom_call" | custom-call | tf_op jit(solution)/shard_map/dynamics/pallas_call | solution.py:468
  105.7 0.0 copy-start
  105.7 2.8 %copy.15 = f32[3,32,32,128]{3,2,1,0:T(8,128)} copy(f32[3,32,32,128]{3,2,1,0:T(8,128)} %get-tuple-element.4) | data formatting | bytes 3145728
  108.5 0.0 copy-done
  108.5 1.1 %copy.16 = f32[3,32,32,128]{3,2,1,0:T(8,128)} copy(f32[3,32,32,128]{3,2,1,0:T(8,128)S(1)} %copy-done) | data formatting | bytes 3145728
Async XLA Ops:
  105.7 2.8 %copy-start = (f32[3,32,32,128]{3,2,1,0:T(8,128)S(1)}, f32[3,32,32,128]{3,2,1,0:T(8,128)}, u32[]{:S(2)}) copy-start(f32[3,32,32,128]{3,2,1,0:T(8,128)} %get-tuple-element.5) | copy-start | bytes 4718596
